TPU v7x, 256 devices: a whole 4x4x8 slice. The times are simulated.
256 devices in a mesh: expert: 64 (over z, y, core), replica: 4 (over x).
Axes of the slice: x: 4, y: 4, z: 8, core: 2. Of those that a mesh axis runs over, the one named last changes fastest.
Arguments:
- inputs: bfloat16 [32768, 2048], P(('expert', 'replica')), may hold values from -16 to 16
- cotangent: bfloat16 [32768, 2048], P(('expert', 'replica')), may hold values from -4 to 4
- routes: int32 [32768, 8], P(('expert', 'replica')), may hold values from 0 to 63, as said below
- router: bfloat16 [2048, 64], replicated, may hold values from -2 to 2
- w_gate: bfloat16 [64, 2048, 384], P('expert'), may hold values from -0.125 to 0.125
- w_up: bfloat16 [64, 2048, 384], P('expert'), may hold values from -0.125 to 0.125
- w_down: bfloat16 [64, 384, 2048], P('expert'), may hold values from -0.3125 to 0.3125
Outputs:
- grad_inputs: bfloat16 [32768, 2048], P(('expert', 'replica'))
- grad_router: float32 [2048, 64], replicated
Inputs may be any that keep to these rules, and one draw needn't show every extreme that they name: `routes`: among the tokens of one device, the same 2 experts as on every device of its replica group (the devices with equal replica index) each fill exactly 56 of the 1024 choices, and every other expert fills at most 16.
All inputs are finite; a program needn't handle non-finite values.
Results may differ from a plain program's by a relative error of at most 0.0075.
Values may be sent and summed in bfloat16 or wider, within the bound.
No kernel may reach another device: no remote copies, remote signals or barrier semaphores. Data moves between devices by JAX's collectives and lax.ppermute only.
A program may use at most 128 MiB of HBM per device.

v0:
```python
import jax
import jax.numpy as jnp
from jax import lax
from jax.sharding import PartitionSpec as P

HELPERS = 5


def from_root(value, axis, source):
    kept = jnp.where(lax.axis_index(axis) == source, value, 0).astype(value.dtype)
    return lax.psum(kept, axis)


def forward_rows(gate_w, up_w, down_w, rows_in):
    gate = jnp.dot(rows_in, gate_w, preferred_element_type=jnp.float32)
    up = jnp.dot(rows_in, up_w, preferred_element_type=jnp.float32)
    sig = jax.nn.sigmoid(gate)
    act = gate * sig
    hidden = (act * up).astype(jnp.bfloat16)
    out = jnp.dot(hidden, down_w, preferred_element_type=jnp.float32)
    return (gate, up, sig, act, out)


def backward_rows(gate_w, up_w, down_w, saved, rows_cot, comb_rows):
    gate, up, sig, act, out = saved
    cot = rows_cot.astype(jnp.float32)
    dcomb = jnp.sum(out * cot, axis=-1).astype(jnp.bfloat16)
    scaled = (comb_rows.astype(jnp.float32)[:, None] * cot).astype(jnp.bfloat16)
    dims = (((1,), (1,)), ((), ()))
    dhid = lax.dot_general(scaled, down_w, dims, preferred_element_type=jnp.float32)
    dgate = (dhid * up * sig * (1.0 + gate * (1.0 - sig))).astype(jnp.bfloat16)
    dup = (dhid * act).astype(jnp.bfloat16)
    dpart = lax.dot_general(dgate, gate_w, dims, preferred_element_type=jnp.float32)
    dpart = dpart + lax.dot_general(dup, up_w, dims, preferred_element_type=jnp.float32)
    return (dpart.astype(jnp.bfloat16), dcomb)


def group_forward(weights, rows_in):
    return forward_rows(weights[0], weights[1], weights[2], rows_in)


def group_backward(weights, saved, rows_cot, comb_rows):
    return backward_rows(weights[0], weights[1], weights[2], saved, rows_cot, comb_rows)


def shards(inputs, cotangent, routes, router, w_gate, w_up, w_down):
    tok_count, width = inputs.shape
    topk = routes.shape[1]
    experts = router.shape[1]
    devices = lax.axis_size("expert")
    mean_rows = tok_count * topk // experts
    cap_guest = mean_rows // 2
    capacity = mean_rows + cap_guest
    hot_count = max(1, experts // 32)
    flat = routes.reshape(-1)
    total = flat.shape[0]
    expert_ids = jnp.arange(experts, dtype=jnp.int32)
    member = (flat[:, None] == expert_ids[None, :]).astype(jnp.int32)
    before = jnp.cumsum(member, axis=0) - member
    rank = jnp.sum(before * member, axis=1)
    counts = jnp.sum(member, axis=0)
    is_hot = (counts > mean_rows).astype(jnp.int32)
    hot_rank = jnp.cumsum(is_hot) - 1
    cold_rank = jnp.cumsum(1 - is_hot) - 1
    helper_slots = jnp.arange(hot_count * HELPERS, dtype=jnp.int32)
    helper_match = (1 - is_hot)[None, :] * (cold_rank[None, :] == helper_slots[:, None]).astype(
        jnp.int32
    )
    helper_device = jnp.sum(helper_match * expert_ids[None, :], axis=1)
    hot_match = is_hot[None, :] * (
        hot_rank[None, :] == jnp.arange(hot_count, dtype=jnp.int32)[:, None]
    ).astype(jnp.int32)
    hot_device = jnp.sum(hot_match * expert_ids[None, :], axis=1)
    row_hot = jnp.sum(member * hot_rank[None, :], axis=1)
    extra = rank - mean_rows
    own_row = extra < 0
    spill = jnp.maximum(extra, 0)
    pick = row_hot * HELPERS + spill // cap_guest
    spill_device = jnp.sum(
        (pick[:, None] == helper_slots[None, :]).astype(jnp.int32) * helper_device[None, :], axis=1
    )
    dest = jnp.where(own_row, flat, spill_device)
    slot = jnp.where(own_row, rank, mean_rows + spill % cap_guest)
    target = dest * capacity + slot
    token_row = jnp.arange(total, dtype=jnp.int32) // topk
    logits = jnp.dot(inputs, router, preferred_element_type=jnp.float32)
    member_f = member.reshape(tok_count, topk, experts).astype(jnp.float32)
    chosen = jnp.sum(logits[:, None, :] * member_f, axis=2)
    top = jnp.max(chosen, axis=1, keepdims=True)
    expo = jnp.exp(chosen - top)
    combine = expo / jnp.sum(expo, axis=1, keepdims=True)
    comb_sent = combine.astype(jnp.bfloat16).reshape(-1)
    send_in = (
        jnp.zeros((devices * capacity, width), jnp.bfloat16)
        .at[target]
        .set(inputs[token_row])
        .reshape(devices, capacity, width)
    )
    send_cot = (
        jnp.zeros((devices * capacity, width), jnp.bfloat16)
        .at[target]
        .set(cotangent[token_row])
        .reshape(devices, capacity, width)
    )
    send_comb = (
        jnp.zeros((devices * capacity,), jnp.bfloat16)
        .at[target]
        .set(comb_sent)
        .reshape(devices, capacity)
    )
    myself = lax.axis_index("expert")
    mine = (expert_ids == myself).astype(jnp.int32)
    my_cold = jnp.sum(mine * cold_rank)
    my_plain = jnp.sum(mine * (1 - is_hot))
    guest_of = jnp.where((my_plain == 1) & (my_cold < hot_count * HELPERS), my_cold // HELPERS, -1)
    own_weights = (w_gate[0], w_up[0], w_down[0])
    guest_gate, guest_up, guest_down = own_weights
    for index in range(hot_count):
        fetched = (
            from_root(w_gate[0], "expert", hot_device[index]),
            from_root(w_up[0], "expert", hot_device[index]),
            from_root(w_down[0], "expert", hot_device[index]),
        )
        taking = guest_of == index
        guest_gate = jnp.where(taking, fetched[0], guest_gate)
        guest_up = jnp.where(taking, fetched[1], guest_up)
        guest_down = jnp.where(taking, fetched[2], guest_down)
    guest_weights = (guest_gate, guest_up, guest_down)

    def own_part(block):
        return block[:, :mean_rows].reshape((devices * mean_rows,) + block.shape[2:])

    def guest_part(block):
        return block[:, mean_rows:].reshape((devices * cap_guest,) + block.shape[2:])

    got_in, got_cot, got_comb = (
        lax.all_to_all(send_in, "expert", split_axis=0, concat_axis=0, tiled=True),
        lax.all_to_all(send_cot, "expert", split_axis=0, concat_axis=0, tiled=True),
        lax.all_to_all(send_comb, "expert", split_axis=0, concat_axis=0, tiled=True),
    )
    saved_own = group_forward(own_weights, own_part(got_in))
    saved_guest = group_forward(guest_weights, guest_part(got_in))
    dx_own, dc_own = group_backward(own_weights, saved_own, own_part(got_cot), own_part(got_comb))
    dx_guest, dc_guest = group_backward(
        guest_weights, saved_guest, guest_part(got_cot), guest_part(got_comb)
    )
    dx_slots = jnp.concatenate(
        [dx_own.reshape(devices, mean_rows, width), dx_guest.reshape(devices, cap_guest, width)],
        axis=1,
    )
    dc_slots = jnp.concatenate(
        [dc_own.reshape(devices, mean_rows), dc_guest.reshape(devices, cap_guest)], axis=1
    )
    back_dx, back_dc = (
        lax.all_to_all(dx_slots, "expert", split_axis=0, concat_axis=0, tiled=True),
        lax.all_to_all(dc_slots, "expert", split_axis=0, concat_axis=0, tiled=True),
    )
    parts = back_dx.reshape(devices * capacity, width)[target].reshape(tok_count, topk, width)
    moe_grad = jnp.sum(parts.astype(jnp.float32), axis=1)
    dcomb = back_dc.reshape(-1)[target].astype(jnp.float32).reshape(tok_count, topk)
    dlogit = combine * (dcomb - jnp.sum(combine * dcomb, axis=1, keepdims=True))
    spread = jnp.sum(dlogit[:, :, None] * member_f, axis=1).astype(jnp.bfloat16)
    back = lax.dot_general(
        spread, router, (((1,), (1,)), ((), ())), preferred_element_type=jnp.float32
    )
    grad_inputs = (moe_grad + back).astype(jnp.bfloat16)
    local_router = lax.dot_general(
        inputs, spread, (((0,), (0,)), ((), ())), preferred_element_type=jnp.float32
    )
    grad_router = lax.psum(local_router, ("expert", "replica"))
    return (grad_inputs, grad_router)


def solution(mesh):
    return jax.shard_map(
        shards,
        mesh=mesh,
        in_specs=(
            P(("expert", "replica"), None),
            P(("expert", "replica"), None),
            P(("expert", "replica"), None),
            P(),
            P("expert", None, None),
            P("expert", None, None),
            P("expert", None, None),
        ),
        out_specs=(P(("expert", "replica"), None), P()),
        check_vma=False,
    )
```

profile of v0, /device:TPU:2, one launch (start us, length us, event | category | flops | bytes accessed | tf_op | source)
XLA Modules:
  0.0 939.8 jit_solution(10307538574417596764)
XLA Ops:
  9.9 18.0 %reduce-window.25 = s32[64,8,128]{2,1,0:T(8,128)S(1)} reduce-window(s32[64,8,128]{2,1,0:T(8,128)S(1)} %fusion.38, s32[]{:T(128)} %constant.82.clone.1), window={size=1x1x128 pad=0_0x0_0x127_0}, to_apply=%region_0.0 | reduce-window | flops 8323072 | bytes 524292 | tf_op jit(solution)/shard_map/reduce-window
  28.7 24.0 %scatter_custom_fusion.2 = bf16[1536,2048]{1,0:T(8,128)(2,1)} fusion(s32[1024]{0:T(1024)S(1)} %bitcast.111, bf16[128,2048]{1,0:T(8,128)(2,1)S(1)} %copy-done, s32[1024]{0:T(1024)S(1)} %broadcast_clamp_fusion.1, bf16[]{:T(256)} %constant.81.clone.1), kind=kCustom, calls=%fused_computation.18 | custom fusion | bytes 6291458 | tf_op jit(solution)/shard_map/scatter | solution.py:96
  52.8 12.3 %all-to-all-start.2 = ((bf16[64,24,2048]{2,1,0:T(8,128)(2,1)}), bf16[64,24,2048]{2,1,0:T(8,128)(2,1)}, u32[]{:S(2)}, u32[]{:S(2)}) async-start(bf16[64,24,2048]{2,1,0:T(8,128)(2,1)} %bitcast.100), calls=%async_computation.2 | async-start | bytes 12582912 | tf_op jit(solution)/shard_map/all_to_all | solution.py:137
  65.1 24.1 %scatter_custom_fusion.1 = bf16[1536,2048]{1,0:T(8,128)(2,1)} fusion(s32[1024]{0:T(1024)S(1)} %bitcast.112, bf16[128,2048]{1,0:T(8,128)(2,1)} %param.8, s32[1024]{0:T(1024)S(1)} %broadcast_clamp_fusion.1, bf16[]{:T(256)} %constant.81.clone.1), kind=kCustom, calls=%fused_computation.20 | custom fusion | bytes 6291968 | tf_op jit(solution)/shard_map/scatter | solution.py:102
  89.2 117.1 %all-to-all-done.2 = bf16[64,24,2048]{2,1,0:T(8,128)(2,1)} async-done(((bf16[64,24,2048]{2,1,0:T(8,128)(2,1)}), bf16[64,24,2048]{2,1,0:T(8,128)(2,1)}, u32[]{:S(2)}, u32[]{:S(2)}) %all-to-all-start.2) | async-done | bytes 6291488 | tf_op jit(solution)/shard_map/all_to_all | solution.py:137
  206.3 6.0 all-to-all-start.1
  214.4 3.5 bitcast_select_fusion.7
  224.0 303.2 %all-reduce.6.cloned.1.call-done = (bf16[2048,384]{1,0:T(8,128)(2,1)}, bf16[2048,384]{1,0:T(8,128)(2,1)}, bf16[384,2048]{1,0:T(8,128)(2,1)}, bf16[384,2048]{1,0:...) async-done(((bf16[2048,384]{1,0:T(8,128)(2,1)}, bf16[2048,384]{1,0:T(8,128)(2,1)}, bf16[384,2048]{1,0:T(8,128)(2,1)}, bf16[384,2048]{1,0:T(8,128)(2,1)}, ...) | async-done | bytes 9437200 | tf_op jit(solution)/shard_map/psum | solution.py:11
  539.3 3.9 fusion.15
  543.2 3.5 fusion.18
  546.7 3.5 fusion.22
  550.2 3.7 fusion.2
  554.1 3.4 slice_convert_fusion
  561.1 7.3 all-to-all-start.4
  568.5 9.6 %all-to-all-done.4 = bf16[64,1,24]{2,1,0:T(2,128)(2,1)S(1)} async-done(((bf16[64,1,24]{2,1,0:T(2,128)(2,1)}), bf16[64,1,24]{2,1,0:T(2,128)(2,1)S(1)}, u32[]{:S(2)}, u32[]{:S(2)}) %all-to-all-start.4) | async-done | bytes 3104 | tf_op jit(solution)/shard_map/all_to_all | solution.py:156
  578.3 6.8 gather_fusion.1
  585.5 7.6 scatter_custom_fusion
  593.2 13.4 %all_to_all.37 = bf16[64,1,24]{2,1,0:T(2,128)(2,1)S(1)} all-to-all(bf16[64,1,24]{2,1,0:T(2,128)(2,1)S(1)} %all_to_all.31), channel_id=1, replica_groups=mesh['expert'=64,'replica'=4] {'expert'}, dimensions={0} | all-to-all | bytes 6144 | tf_op jit(solution)/shard_map/all_to_all | solution.py:139
  624.3 3.8 pad_maximum_fusion
  628.1 5.7 all-to-all-start.3
  635.2 141.6 %all-to-all-done.3 = bf16[64,24,2048]{2,1,0:T(8,128)(2,1)} async-done(((bf16[64,24,2048]{2,1,0:T(8,128)(2,1)}), bf16[64,24,2048]{2,1,0:T(8,128)(2,1)}, u32[]{:S(2)}, u32[]{:S(2)}) %all-to-all-start.3) | async-done | bytes 6291488 | tf_op jit(solution)/shard_map/all_to_all | solution.py:155
  776.8 12.4 %gather_fusion = bf16[1024,2048]{1,0:T(8,128)(2,1)} fusion(bf16[1536,2048]{1,0:T(8,128)(2,1)} %bitcast.21, s32[1024]{0:T(1024)S(1)} %broadcast_clamp_fusion), kind=kCustom, calls=%fused_computation.2 | custom fusion | bytes 8392704 | tf_op jit(solution)/shard_map/gather | solution.py:158
  789.2 5.1 convert_reduce_fusion
  795.4 135.3 %all-reduce.4.cloned.1.call-done = f32[2048,64]{0,1:T(8,128)} async-done(((f32[2048,64]{0,1:T(8,128)}), f32[2048,64]{0,1:T(8,128)}) %all-reduce.4.cloned.1.call-update) | async-done | bytes 524304 | tf_op jit(solution)/shard_map/psum | solution.py:170
  (127 shorter events, 45.9 us)
Async XLA Ops:
  7.2 21.6 %copy-start = (bf16[128,2048]{1,0:T(8,128)(2,1)S(1)}, bf16[128,2048]{1,0:T(8,128)(2,1)}, u32[]{:S(2)}) copy-start(bf16[128,2048]{1,0:T(8,128)(2,1)} %param.7) | copy-start | bytes 1572868
  52.8 153.5 %all-to-all-start.2 = ((bf16[64,24,2048]{2,1,0:T(8,128)(2,1)}), bf16[64,24,2048]{2,1,0:T(8,128)(2,1)}, u32[]{:S(2)}, u32[]{:S(2)}) async-start(bf16[64,24,2048]{2,1,0:T(8,128)(2,1)} %bitcast.100), calls=%async_computation.2 | async-start | bytes 12582912 | tf_op jit(solution)/shard_map/all_to_all | solution.py:137
  206.3 343.9 %all-to-all-start.1 = ((bf16[64,24,2048]{2,1,0:T(8,128)(2,1)}), bf16[64,24,2048]{2,1,0:T(8,128)(2,1)}, u32[]{:S(2)}, u32[]{:S(2)}) async-start(bf16[64,24,2048]{2,1,0:T(8,128)(2,1)} %bitcast.99), calls=%async_computation.1 | async-start | bytes 12582912 | tf_op jit(solution)/shard_map/all_to_all | solution.py:138
  212.3 314.9 %all-reduce.6.cloned.1.call-start = ((), (), s32[]{:S(2)}) async-start(), calls=%async_computation.6 | async-start | bytes 18874368 | tf_op jit(solution)/shard_map/psum | solution.py:11
  214.4 3.5 copy-start.1
  214.4 3.5 copy-start.2
  220.7 3.0 copy-start.21
  220.7 3.3 copy-start.23
  527.2 2.8 copy-start.19
  527.2 3.4 copy-start.20
  529.5 6.9 copy-start.12
  530.7 2.4 copy-start.18
  533.4 6.0 copy-start.10
  539.3 3.9 copy-start.3
  554.1 3.5 copy-start.5
  554.1 3.5 copy-start.8
  554.1 3.6 copy-start.14
  561.1 16.9 %all-to-all-start.4 = ((bf16[64,1,24]{2,1,0:T(2,128)(2,1)}), bf16[64,1,24]{2,1,0:T(2,128)(2,1)S(1)}, u32[]{:S(2)}, u32[]{:S(2)}) async-start(bf16[64,1,24]{2,1,0:T(2,128)(2,1)} %copy.65), calls=%async_computation.4 | async-start | bytes 65536 | tf_op jit(solution)/shard_map/all_to_all | solution.py:156
  607.0 3.1 copy-start.9
  610.1 2.4 copy-start.16
  612.4 3.1 copy-start.13
  612.4 3.1 copy-start.22
  628.1 148.7 %all-to-all-start.3 = ((bf16[64,24,2048]{2,1,0:T(8,128)(2,1)}), bf16[64,24,2048]{2,1,0:T(8,128)(2,1)}, u32[]{:S(2)}, u32[]{:S(2)}) async-start(bf16[64,24,2048]{2,1,0:T(8,128)(2,1)} %pad_maximum_fusion), calls=%async_computation.3 | async-start | bytes 12582912 | tf_op jit(solution)/shard_map/all_to_all | solution.py:155
  633.8 296.9 %all-reduce.4.cloned.1.call-start = ((), (), s32[]{:S(2)}) async-start(), calls=%async_computation.5 | async-start | bytes 1048576 | tf_op jit(solution)/shard_map/psum | solution.py:170
  (6 other events, 11.4 us)
Sparse Core Ops, SparseCore 0:
  220.8 306.3 all-reduce.5
  641.5 289.0 all-reduce.3
where the time goes:
time: 949 us; the launch traced here: 940 us
  waiting for transfers between devices  707 us (74%)
  local copies, waits for them, and re-layouts  87.6 us (9%)
  other arithmetic  45.7 us (5%)
  matrix products  35.5 us (4%)
  starting transfers between devices  31.7 us (3%)
  between operations  19.2 us (2%)
  blocking collectives  13.4 us (1%)
    psum x1, waiting for transfers between devices, from_root(): return lax.psum(kept, axis)  303 us
    all_to_all x1, waiting for transfers between devices, shards(): lax.all_to_all(dx_slots, 'expert', split_axis=0, concat_axis=0, tiled=True)  142 us
    psum x1, waiting for transfers between devices, shards(): grad_router = lax.psum(local_router, ('expert', 'replica'))  135 us
    all_to_all x1, waiting for transfers between devices, shards(): lax.all_to_all(send_in, 'expert', split_axis=0, concat_axis=0, tiled=True)  117 us
    scatter x1, local copies, waits for them, and re-layouts, shards(): send_cot = jnp.zeros((devices * capacity, width), jnp.bfloat16).at[target...  24.1 us
    scatter x1, local copies, waits for them, and re-layouts, shards(): send_in = jnp.zeros((devices * capacity, width), jnp.bfloat16).at[target]...  24 us
  transfers between devices with their start and end apart: 6, of which 5 were waited for; matrix products, arithmetic and copies ran while one was open for 8% of the time, Pallas kernels for 0%

commit v1 on v0

v1 whole, which is shorter than its diff:
```python
import jax
import jax.numpy as jnp
from jax import lax
from jax.sharding import Mesh, PartitionSpec as P

NZ, NY, NC, NX = 8, 4, 2, 4
SLICE = NY * NC
EXPERTS = NZ * SLICE
CAP = 16
HOT = 2
HOT_CAP = 64
BF = jnp.bfloat16
F32 = jnp.float32
ROWS = ("z", "y", "c", "x")
GROUP = ("z", "y", "c")
PLANE = ("y", "c")


def exchange(value, axes):
    return lax.all_to_all(value, axes, split_axis=0, concat_axis=0, tiled=True)


def spread_out(value, axes, count):
    return exchange(jnp.broadcast_to(value[None], (count,) + value.shape), axes)


def dot(a, b, dims):
    return lax.dot_general(a, b, (dims, ((), ())), preferred_element_type=F32)


def selectors(code, weight, slots):
    ids = lax.broadcasted_iota(jnp.int32, (1, slots, 1), 1)
    hits = code[:, :, None, :] == ids[:, None]
    chosen = jnp.sum(hits.astype(F32), axis=1).astype(BF)
    weighted = jnp.sum(jnp.where(hits, weight[:, :, None, :], 0.0), axis=1).astype(BF)
    return chosen, weighted


def around(value, axis, size):
    turned = [value] + [
        lax.ppermute(value, axis, [(i, (i - shift) % size) for i in range(size)])
        for shift in range(1, size)
    ]
    return jnp.roll(jnp.stack(turned), lax.axis_index(axis), axis=0)


def earlier(count):
    size = count.shape[-1]
    rows = lax.broadcasted_iota(jnp.int32, (size, size), 0)
    cols = lax.broadcasted_iota(jnp.int32, (size, size), 1)
    mask = (rows < cols).astype(BF)
    before = lax.dot_general(
        count.astype(BF), mask, (((count.ndim - 1,), (0,)), ((), ())), preferred_element_type=F32
    )
    return before.astype(jnp.int32)


def forward(gate, up):
    sig = jax.nn.sigmoid(gate)
    act = gate * sig
    slope = up * sig * (1.0 + gate * (1.0 - sig))
    return lax.reduce_precision(act * up, 8, 7), act, slope


def backward(saved, dhid):
    hidden, act, slope = saved
    dcomb = lax.reduce_precision(jnp.sum(hidden * dhid, axis=-1), 8, 7)
    return (dhid * slope).astype(BF), (dhid * act).astype(BF), dcomb


def hot_expert(rows_in, rows_cot, mine, other, side):
    half = rows_in.shape[1] // 2
    ff = mine.shape[1] // 3

    def halves(rows):
        low, high = rows[:, :half], rows[:, half:]
        return jnp.where(side == 0, low, high), jnp.where(side == 0, high, low)

    in_mine, in_other = halves(rows_in)
    cot_mine, cot_other = halves(rows_cot)
    both = dot(in_mine, mine[:, : 2 * ff], ((1,), (0,))) + dot(
        in_other, other[:, : 2 * ff], ((1,), (0,))
    )
    saved = forward(both[:, :ff], both[:, ff:])
    dhid = dot(cot_mine, mine[:, 2 * ff :], ((1,), (0,))) + dot(
        cot_other, other[:, 2 * ff :], ((1,), (0,))
    )
    dgate, dup, dcomb = backward(saved, dhid)
    grads = jnp.concatenate([dgate, dup], axis=1)
    dx_mine = dot(grads, mine[:, : 2 * ff], ((1,), (1,))).astype(BF)
    dx_other = dot(grads, other[:, : 2 * ff], ((1,), (1,))).astype(BF)
    low = jnp.where(side == 0, dx_mine, dx_other)
    high = jnp.where(side == 0, dx_other, dx_mine)
    return jnp.concatenate([low, high], axis=1), dcomb


def shards(inputs, cotangent, routes, router, w_gate, w_up, w_down):
    tok, width = inputs.shape
    topk = routes.shape[1]
    zi, ci, xi = lax.axis_index("z"), lax.axis_index("c"), lax.axis_index("x")
    rows = SLICE * NZ * CAP

    routes_t = routes.T
    in_all = lax.all_gather(inputs, "z")

    part = width // (NC * NZ * NY * NX)

    def quarter(weights):
        blocks = weights.reshape(NC, NZ, NY, NX, part, weights.shape[1])
        return lax.dynamic_index_in_dim(blocks, xi, axis=3, keepdims=False)

    packed = jnp.concatenate([quarter(w_gate[0]), quarter(w_up[0]), quarter(w_down[0].T)], axis=-1)
    cols = packed.shape[-1]
    pieces = exchange(packed.transpose(2, 0, 1, 3, 4).reshape(SLICE, NZ, part, cols), PLANE)

    member = routes_t[:, None, :] == lax.broadcasted_iota(jnp.int32, (1, EXPERTS, 1), 1)
    member_f = member.astype(F32)
    count = jnp.sum(member.astype(jnp.int32), axis=0)
    before = earlier(count)
    is_hot = (jnp.sum(count, axis=1) > CAP).astype(jnp.int32)
    ids = jnp.arange(EXPERTS, dtype=jnp.int32)
    hot_rank = jnp.sum(jnp.where(ids[None, :] < ids[:, None], is_hot[None, :], 0), axis=1)
    hot_pick = is_hot[None, :] * (hot_rank[None, :] == jnp.arange(HOT)[:, None]).astype(jnp.int32)
    hot_id = jnp.sum(hot_pick * ids[None, :], axis=1)
    ks = jnp.arange(topk)
    same = (routes_t[:, None, :] == routes_t[None, :, :]) & (ks[None, :] < ks[:, None])[:, :, None]
    rank = jnp.sum(jnp.where(member, before[None], 0), axis=1) + jnp.sum(same.astype(jnp.int32), axis=1)
    hot_slot = jnp.sum(jnp.where(routes_t[None] == hot_id[:, None, None], 1 + jnp.arange(HOT)[:, None, None], 0), axis=0)
    code = jnp.where(hot_slot > 0, -1, routes_t * CAP + rank)
    hot_code = jnp.where(hot_slot > 0, (hot_slot - 1) * HOT_CAP + rank, -1)
    logits = dot(router, inputs, ((0,), (1,)))
    chosen = jnp.sum(logits[None] * member_f, axis=1)
    expo = jnp.exp(chosen - jnp.max(chosen, axis=0, keepdims=True))
    combine = expo / jnp.sum(expo, axis=0, keepdims=True)
    comb_sent = combine.astype(BF).astype(F32)

    ring = spread_out(jnp.concatenate([code.astype(F32), comb_sent], axis=0), "z", NZ)
    local = ring[:, :topk].astype(jnp.int32) - zi * SLICE * CAP
    pick, pick_comb = selectors(local, ring[:, topk:], SLICE * CAP)
    hot_ids = [hot_id] + [
        lax.ppermute(hot_id, "x", [(i, (i - shift) % NX) for i in range(NX)]) for shift in range(1, NX)
    ]
    in_all, pick, pieces, hot_ids, later_cot = lax.optimization_barrier(
        (in_all, pick, pieces, hot_ids, cotangent)
    )
    cot_all = lax.all_gather(later_cot, "z")

    sources = zi * SLICE + jnp.arange(SLICE)
    got = []
    for shift in range(NX):
        wanted = (sources[None, :] == hot_ids[shift][:, None])[:, :, None, None, None]
        held = jnp.sum(jnp.where(wanted, pieces[None], jnp.zeros((), BF)), axis=1, dtype=BF)
        if shift:
            held = lax.ppermute(held, "x", [(i, (i + shift) % NX) for i in range(NX)])
        got.append(held)
    quarters = jnp.roll(jnp.stack([got[-j % NX] for j in range(NX)]), xi, axis=0)
    held = quarters.transpose(2, 1, 0, 3, 4).reshape(NZ, HOT * NX * part, cols)

    def to_experts(all_rows):
        sent = lax.dot_general(pick, all_rows, (((2,), (1,)), ((0,), (0,))), preferred_element_type=F32)
        sent = sent.astype(BF).reshape(NZ, SLICE, CAP, width).transpose(1, 0, 2, 3)
        return exchange(sent, PLANE).reshape(rows, width)

    rows_in = to_experts(in_all)
    rows_in, held, cot_all = lax.optimization_barrier((rows_in, held, cot_all))
    rows_cot = to_experts(cot_all)
    held = lax.psum_scatter(held, "z", scatter_dimension=0).reshape(HOT, NX * part, cols)
    held = around(held, "y", NY).transpose(1, 0, 2, 3).reshape(HOT, NY * NX * part, cols)
    saved = forward(dot(rows_in, w_gate[0], ((1,), (0,))), dot(rows_in, w_up[0], ((1,), (0,))))
    rows_cot, saved, held = lax.optimization_barrier((rows_cot, saved, held))
    dgate, dup, dcomb_rows = backward(saved, dot(rows_cot, w_down[0], ((1,), (1,))))
    dpart = dot(dgate, w_gate[0], ((1,), (1,))) + dot(dup, w_up[0], ((1,), (1,)))
    dpart = dpart.astype(BF)
    dcomb_rows = dcomb_rows.reshape(SLICE, NZ, CAP).transpose(1, 0, 2).reshape(EXPERTS, CAP)
    dcomb_rows = jnp.pad(dcomb_rows, ((0, 0), (0, 128 - CAP))).reshape(EXPERTS, 1, 128)
    dcomb_slots = exchange(dcomb_rows, GROUP)
    dpart, dcomb_slots = lax.optimization_barrier((dpart, dcomb_slots))

    mine = lax.all_gather(held, "z", axis=1, tiled=True)
    back_rows = exchange(dpart.reshape(SLICE, NZ, CAP, width), PLANE)
    back_rows, mine = lax.optimization_barrier((back_rows, mine))
    other = lax.ppermute(mine, "c", [(0, 1), (1, 0)])
    hot_rows, hot_rows_comb = selectors(hot_code[None], comb_sent[None], HOT * HOT_CAP)
    hot_in = dot(hot_rows[0], inputs, ((1,), (0,))).astype(BF).reshape(HOT, HOT_CAP, width)
    hot_cot = dot(hot_rows[0], cotangent, ((1,), (0,))).astype(BF).reshape(HOT, HOT_CAP, width)
    hot_dx, hot_dcomb = [], []
    for index in range(HOT):
        dx, dcomb = hot_expert(hot_in[index], hot_cot[index], mine[index], other[index], ci)
        hot_dx.append(dx)
        hot_dcomb.append(dcomb)
    hot_grad = dot(hot_rows_comb[0], jnp.concatenate(hot_dx, axis=0), ((0,), (0,)))

    back_rows = back_rows.transpose(1, 0, 2, 3).reshape(NZ, SLICE * CAP, width)
    partial = lax.dot_general(
        pick_comb, back_rows, (((1,), (1,)), ((0,), (0,))), preferred_element_type=F32
    )
    cold_grad = lax.psum_scatter(partial.astype(BF), "z", scatter_dimension=0)

    hot_pick_f = hot_pick.astype(F32)
    cold = 1.0 - jnp.sum(hot_pick_f, axis=0)
    dcomb_slots = dcomb_slots[:, 0, :HOT_CAP] * cold[:, None]
    dcomb_slots = dcomb_slots + jnp.sum(
        hot_pick_f[:, :, None] * jnp.stack(hot_dcomb)[:, None, :], axis=0
    )
    by_rank = lax.dot_general(
        member.astype(BF), dcomb_slots.astype(BF), (((1,), (0,)), ((), ())), preferred_element_type=F32
    )
    ranked = rank[:, None, :] == lax.broadcasted_iota(jnp.int32, (1, HOT_CAP, 1), 1)
    dcomb = jnp.sum(jnp.where(ranked, by_rank.transpose(0, 2, 1), 0.0), axis=1)
    dlogit = combine * (dcomb - jnp.sum(combine * dcomb, axis=0, keepdims=True))
    spread = jnp.sum(dlogit[:, None, :] * member_f, axis=0).astype(BF)
    devices = NZ * NY * NC * NX
    local_router = dot(spread, inputs, ((1,), (0,)))
    lanes = EXPERTS * width // (devices * 4)
    shares = exchange(local_router.reshape(devices, 4, lanes), ROWS)
    total = jnp.sum(shares, axis=0)
    grad_router = spread_out(total, ROWS, devices).reshape(EXPERTS, width).T

    back = dot(spread, router, ((0,), (1,)))
    grad_inputs = (cold_grad.astype(F32) + hot_grad + back).astype(BF)
    return grad_inputs, grad_router


def solution(mesh):
    fine = Mesh(mesh.devices.reshape(NZ, NY, NC, NX), ROWS)
    tokens = P(ROWS, None)
    experts = P(GROUP, None, None)
    return jax.shard_map(
        shards,
        mesh=fine,
        in_specs=(tokens, tokens, tokens, P(), experts, experts, experts),
        out_specs=(tokens, P()),
        check_vma=False,
    )
```

time: 949 us -> 376 us (0.40)
  waiting for transfers between devices: 707 us -> 131 us
  blocking collectives: 13.4 us -> 88.8 us
  local copies, waits for them, and re-layouts: 87.6 us -> 27.5 us
  other arithmetic: 45.7 us -> 10.3 us
  starting transfers between devices: 31.7 us -> 51.1 us
  matrix products: 35.5 us -> 49.4 us
    psum x2 -> x0, waiting for transfers between devices: 438 us -> none  [the longest x1 303 us: from_root(): return lax.psum(kept, axis)]
    all_to_all x4 -> x6, waiting for transfers between devices: 268 us -> 64.6 us  [exchange(): return lax.all_to_all(value, axes, split_axis=0, concat_axis=0, tiled=True)]
    all_to_all x1 -> x2, blocking collectives: 13.4 us -> 88.8 us  [exchange(): return lax.all_to_all(value, axes, split_axis=0, concat_axis=0, tiled=True)]
    scatter x3 -> x0, local copies, waits for them, and re-layouts: 55.7 us -> none  [the longest x1 24.1 us: shards(): send_cot = jnp.zeros((devices * capacity, width), jnp.bfloat16).at[target...]
    ppermute x0 -> x10, waiting for transfers between devices: none -> 38.2 us  [the longest x3 24.8 us: around(): lax.ppermute(value, axis, [(i, (i - shift) % size) for i in range(size)])]
    gather x2 -> x0, local copies, waits for them, and re-layouts: 19.2 us -> none  [the longest x1 12.4 us: shards(): back_dx.reshape(devices * capacity, width)[target]]
    another operation x5 -> x1, other arithmetic: 18.4 us -> 0.01 us  [shards(): jnp.stack(hot_dcomb)[:, None, :]]
    all_gather x0 -> x3, waiting for transfers between devices: none -> 14.5 us  [the longest x1 14.5 us: shards(): in_all = lax.all_gather(inputs, 'z')]
  transfers between devices with their start and end apart: 6 -> 21, of which waited for: 5 -> 13; matrix products, arithmetic and copies ran while one was open for 8% -> 22% of each run, Pallas kernels for 0% -> 0%
where the time goes in v1:
time: 376 us; the launch traced here: 373 us
  waiting for transfers between devices  131 us (35%)
  blocking collectives  88.8 us (24%)
  starting transfers between devices  51.1 us (14%)
  matrix products  49.4 us (13%)
  local copies, waits for them, and re-layouts  27.5 us (7%)
  between operations  14.4 us (4%)
  other arithmetic  10.3 us (3%)
    all_to_all x2, blocking collectives, exchange(): return lax.all_to_all(value, axes, split_axis=0, concat_axis=0, tiled=True)  88.8 us
    all_to_all x6, waiting for transfers between devices, exchange(): return lax.all_to_all(value, axes, split_axis=0, concat_axis=0, tiled=True)  64.6 us
    dot_general x23, matrix products, dot(): return lax.dot_general(a, b, (dims, ((), ())), preferred_element_type=F32)  38.8 us
    all_to_all x6, starting transfers between devices, exchange(): return lax.all_to_all(value, axes, split_axis=0, concat_axis=0, tiled=True)  36.6 us
    ppermute x3, waiting for transfers between devices, around(): lax.ppermute(value, axis, [(i, (i - shift) % size) for i in range(size)])  24.8 us
    all_gather x1, waiting for transfers between devices, shards(): in_all = lax.all_gather(inputs, 'z')  14.5 us
    reduce_scatter x1, waiting for transfers between devices, shards(): lax.psum_scatter(held, 'z', scatter_dimension=0)  13.4 us
    ppermute x3, waiting for transfers between devices, shards(): held = lax.ppermute(held, 'x', [(i, (i + shift) % NX) for i in range(NX)])  13.1 us
  transfers between devices with their start and end apart: 21, of which 13 were waited for; matrix products, arithmetic and copies ran while one was open for 22% of the time, Pallas kernels for 0%

profile of v1, /device:TPU:2, one launch (start us, length us, event | category | flops | bytes accessed | tf_op | source)
XLA Modules:
  0.0 373.0 jit_solution(5595504242502044610)
XLA Ops:
  15.1 8.5 %all-to-all-start = ((f32[8,16,128]{2,1,0:T(8,128)}), f32[8,16,128]{2,1,0:T(8,128)S(1)}, u32[]{:S(2)}, u32[]{:S(2)}) async-start(f32[8,16,128]{2,1,0:T(8,128)} %broadcast_in_dim.178), calls=%async_computation | async-start | bytes 131072 | tf_op jit(solution)/shard_map/all_to_all | solution.py:20
  28.0 4.4 %all-to-all-done = f32[8,16,128]{2,1,0:T(8,128)S(1)} async-done(((f32[8,16,128]{2,1,0:T(8,128)}), f32[8,16,128]{2,1,0:T(8,128)S(1)}, u32[]{:S(2)}, u32[]{:S(2)}) %all-to-all-start) | async-done | bytes 65568 | tf_op jit(solution)/shard_map/all_to_all | solution.py:20
  32.4 4.5 %all-to-all-start.1 = ((bf16[8,8,8,1152]{3,2,1,0:T(8,128)(2,1)}), bf16[8,8,8,1152]{3,2,1,0:T(8,128)(2,1)S(1)}, u32[]{:S(2)}, u32[]{:S(2)}) async-start(bf16[8,8,8,1152]{3,2,1,0:T(8,128)(2,1)} %bitcast.11), calls=%async_computation.1 | async-start | bytes 2359296 | tf_op jit(solution)/shard_map/all_to_all | solution.py:20
  43.5 10.7 %all-to-all-done.1 = bf16[8,8,8,1152]{3,2,1,0:T(8,128)(2,1)S(1)} async-done(((bf16[8,8,8,1152]{3,2,1,0:T(8,128)(2,1)}), bf16[8,8,8,1152]{3,2,1,0:T(8,128)(2,1)S(1)}, u32[]{:S(2)}, u32[]{:S(2)}) %all-to-all-start.1) | async-done | bytes 1179680 | tf_op jit(solution)/shard_map/all_to_all | solution.py:20
  54.3 14.5 %all-gather.8.cloned.1.call-done = bf16[1024,2048]{1,0:T(8,128)(2,1)} async-done(((bf16[128,2048]{1,0:T(8,128)(2,1)}), bf16[1024,2048]{1,0:T(8,128)(2,1)}) %all-gather.8.cloned.1.call-update) | async-done | bytes 4194320 | tf_op jit(solution)/shard_map/all_gather | solution.py:104
  72.6 3.4 convolution_convert_fusion.2
  78.3 4.7 %all-to-all-start.2 = ((bf16[8,8,16,2048]{3,2,1,0:T(8,128)(2,1)}), bf16[8,8,16,2048]{3,2,1,0:T(8,128)(2,1)}, u32[]{:S(2)}, u32[]{:S(2)}) async-start(bf16[8,8,16,2048]{3,2,1,0:T(8,128)(2,1)} %bitcast.154), calls=%async_computation.2 | async-start | bytes 8388608 | tf_op jit(solution)/shard_map/all_to_all | solution.py:20
  87.4 6.8 %collective-permute-done.4 = bf16[2,8,8,1152]{3,2,1,0:T(8,128)(2,1)S(1)} collective-permute-done((bf16[2,8,8,1152]{3,2,1,0:T(8,128)(2,1)}, bf16[2,8,8,1152]{3,2,1,0:T(8,128)(2,1)S(1)}, u32[]{:S(2)}, u32[]{:S(2)}) %collective-permute-start.4) | collective-permute-done | bytes 294944 | tf_op jit(solution)/shard_map/ppermute | solution.py:154
  94.2 6.3 %collective-permute-done.5 = bf16[2,8,8,1152]{3,2,1,0:T(8,128)(2,1)S(1)} collective-permute-done((bf16[2,8,8,1152]{3,2,1,0:T(8,128)(2,1)S(1)}, bf16[2,8,8,1152]{3,2,1,0:T(8,128)(2,1)S(1)}, u32[]{:S(2)}, u32[]{:S(2)}) %collective-permute-start.5) | collective-permute-done | bytes 294944 | tf_op jit(solution)/shard_map/ppermute | solution.py:154
  102.0 30.7 %all-to-all-done.2 = bf16[8,8,16,2048]{3,2,1,0:T(8,128)(2,1)} async-done(((bf16[8,8,16,2048]{3,2,1,0:T(8,128)(2,1)}), bf16[8,8,16,2048]{3,2,1,0:T(8,128)(2,1)}, u32[]{:S(2)}, u32[]{:S(2)}) %all-to-all-start.2) | async-done | bytes 4194336 | tf_op jit(solution)/shard_map/all_to_all | solution.py:20
  132.8 3.4 convolution_convert_fusion.1
  138.5 4.7 %all-to-all-start.3 = ((bf16[8,8,16,2048]{3,2,1,0:T(8,128)(2,1)}), bf16[8,8,16,2048]{3,2,1,0:T(8,128)(2,1)}, u32[]{:S(2)}, u32[]{:S(2)}) async-start(bf16[8,8,16,2048]{3,2,1,0:T(8,128)(2,1)} %bitcast.153), calls=%async_computation.3 | async-start | bytes 8388608 | tf_op jit(solution)/shard_map/all_to_all | solution.py:20
  143.3 4.5 %fusion.4 = f32[1024,384]{1,0:T(8,128)S(1)} fusion(bf16[1024,2048]{1,0:T(8,128)(2,1)} %bitcast.14, bf16[1,2048,384]{2,1,0:T(8,128)(2,1)S(1)} %copy-done.3), kind=kOutput, calls=%fused_computation.25 | convolution fusion | flops 1610612736 | bytes 7340032 | tf_op jit(solution)/shard_map/dot_general | solution.py:28
  147.8 7.3 %add_multiply_fusion = (f32[1024,384]{1,0:T(8,128)}, f32[1024,384]{1,0:T(8,128)}, f32[1024,384]{1,0:T(8,128)}) fusion(f32[1024,384]{1,0:T(8,128)S(1)} %fusion.4, bf16[1024,2048]{1,0:T(8,128)(2,1)} %bitcast.14, bf16[1,2048,384]{2,1,0:T(8,128)(2,1)S(1)} %copy-done), kind=kOutput, calls=%fused_computation.34 | convolution fusion | flops 1614938112 | bytes 12058624 | tf_op jit(solution)/shard_map/dot_general | solution.py:28
  155.1 13.4 %reduce-scatter.3.cloned.1.call-done = bf16[1,64,1152]{2,1,0:T(8,128)(2,1)} async-done(((bf16[8,64,1152]{2,1,0:T(8,128)(2,1)}), bf16[1,64,1152]{2,1,0:T(8,128)(2,1)}) %reduce-scatter.3.cloned.1.call-update) | async-done | bytes 147472 | tf_op jit(solution)/shard_map/reduce_scatter | solution.py:167
  174.0 21.0 %collective-permute-done.6 = bf16[2,32,1152]{2,1,0:T(8,128)(2,1)S(1)} collective-permute-done((bf16[2,32,1152]{2,1,0:T(8,128)(2,1)}, bf16[2,32,1152]{2,1,0:T(8,128)(2,1)S(1)}, u32[]{:S(2)}, u32[]{:S(2)}) %collective-permute-start.6) | collective-permute-done | bytes 147488 | tf_op jit(solution)/shard_map/ppermute | solution.py:41
  200.8 5.5 %multiply_reduce_fusion = (f32[1024]{0:T(1024)S(1)}, f32[1024,384]{1,0:T(8,128)S(1)}) fusion(f32[1024,384]{1,0:T(8,128)} %get-tuple-element.36, bf16[1024,2048]{1,0:T(8,128)(2,1)} %bitcast.24, bf16[1,384,2048]{2,1,0:T(8,128)(2,1)} %param.13), kind=kOutput, calls=%fused_computation.31 | convolution fusion | flops 1611398144 | bytes 8916992 | tf_op jit(solution)/shard_map/dot_general | solution.py:28
  207.0 6.2 %all-to-all-start.4 = ((f32[64,1,128]{2,1,0:T(1,128)}), f32[64,1,128]{2,1,0:T(1,128)S(1)}, u32[]{:S(2)}, u32[]{:S(2)}) async-start(f32[64,1,128]{2,1,0:T(1,128)} %bitcast.43), calls=%async_computation.5 | async-start | bytes 65536 | tf_op jit(solution)/shard_map/all_to_all | solution.py:20
  213.5 3.9 %fusion.6 = f32[1024,2048]{1,0:T(8,128)S(1)} fusion(bf16[1,2048,384]{2,1,0:T(8,128)(2,1)S(1)} %copy-done, f32[1024,384]{1,0:T(8,128)S(1)} %get-tuple-element.78, f32[1024,384]{1,0:T(8,128)} %get-tuple-element.34), kind=kOutput, calls=%fused_computation.27 | convolution fusion | flops 1611399168 | bytes 13107200 | tf_op jit(solution)/shard_map/dot_general | solution.py:28
  217.4 4.4 %add_convert_fusion = bf16[1024,2048]{1,0:T(8,128)(2,1)} fusion(f32[1024,2048]{1,0:T(8,128)S(1)} %fusion.6, bf16[1,2048,384]{2,1,0:T(8,128)(2,1)S(1)} %copy-done.4, f32[1024,384]{1,0:T(8,128)S(1)} %get-tuple-element.78, f32[1024,384]{1,0:T(8,128)S(1)} %copy-done.12), kind=kOutput, calls=%fused_computation | convolution fusion | flops 1615593472 | bytes 17301504 | tf_op jit(solution)/shard_map/dot_general | solution.py:28
  223.0 54.8 %all_to_all.40 = bf16[8,8,16,2048]{3,2,1,0:T(8,128)(2,1)} all-to-all(bf16[8,8,16,2048]{3,2,1,0:T(8,128)(2,1)} %bitcast.159), channel_id=1, replica_groups=mesh['z'=8,'y'=4,'c'=2,'x'=4] {'y','c'}, dimensions={0} | all-to-all | bytes 8388608 | tf_op jit(solution)/shard_map/all_to_all | solution.py:20
  296.6 34.0 %all_to_all.41 = f32[256,4,128]{2,1,0:T(4,128)S(1)} all-to-all(f32[256,4,128]{2,1,0:T(4,128)S(1)} %reshape.389), channel_id=1, replica_groups=mesh['z'=8,'y'=4,'c'=2,'x'=4] {'z','y','c','x'}, dimensions={0} | all-to-all | bytes 1048576 | tf_op jit(solution)/shard_map/all_to_all | solution.py:20
  331.8 8.0 %all-to-all-start.7 = ((f32[256,4,128]{2,1,0:T(4,128)}), f32[256,4,128]{2,1,0:T(4,128)S(1)}, u32[]{:S(2)}, u32[]{:S(2)}) async-start(f32[256,4,128]{2,1,0:T(4,128)} %broadcast_in_dim.189), calls=%async_computation.9 | async-start | bytes 1048576 | tf_op jit(solution)/shard_map/all_to_all | solution.py:20
  345.4 17.6 %all-to-all-done.7 = f32[256,4,128]{2,1,0:T(4,128)S(1)} async-done(((f32[256,4,128]{2,1,0:T(4,128)}), f32[256,4,128]{2,1,0:T(4,128)S(1)}, u32[]{:S(2)}, u32[]{:S(2)}) %all-to-all-start.7) | async-done | bytes 524320 | tf_op jit(solution)/shard_map/all_to_all | solution.py:20
  (157 shorter events, 75.2 us)
Async XLA Ops:
  7.2 18.3 %copy-start = (bf16[1,2048,384]{2,1,0:T(8,128)(2,1)S(1)}, bf16[1,2048,384]{2,1,0:T(8,128)(2,1)}, u32[]{:S(2)}) copy-start(bf16[1,2048,384]{2,1,0:T(8,128)(2,1)} %param.11) | copy-start | bytes 4718596
  7.2 61.6 %all-gather.8.cloned.1.call-start = ((), (), s32[]{:S(2)}) async-start(), calls=%async_computation.13 | async-start | bytes 4718592 | tf_op jit(solution)/shard_map/all_gather | solution.py:104
  15.1 17.3 %all-to-all-start = ((f32[8,16,128]{2,1,0:T(8,128)}), f32[8,16,128]{2,1,0:T(8,128)S(1)}, u32[]{:S(2)}, u32[]{:S(2)}) async-start(f32[8,16,128]{2,1,0:T(8,128)} %broadcast_in_dim.178), calls=%async_computation | async-start | bytes 131072 | tf_op jit(solution)/shard_map/all_to_all | solution.py:20
  32.4 21.9 %all-to-all-start.1 = ((bf16[8,8,8,1152]{3,2,1,0:T(8,128)(2,1)}), bf16[8,8,8,1152]{3,2,1,0:T(8,128)(2,1)S(1)}, u32[]{:S(2)}, u32[]{:S(2)}) async-start(bf16[8,8,8,1152]{3,2,1,0:T(8,128)(2,1)} %bitcast.11), calls=%async_computation.1 | async-start | bytes 2359296 | tf_op jit(solution)/shard_map/all_to_all | solution.py:20
  36.9 95.8 %all-gather.10.cloned.1.call-start = ((), (), s32[]{:S(2)}) async-start(), calls=%async_computation.14 | async-start | bytes 4718592 | tf_op jit(solution)/shard_map/all_gather | solution.py:146
  36.9 6.4 %collective-permute-start = (s32[2]{0:T(128)S(1)}, s32[2]{0:T(128)S(1)}, u32[]{:S(2)}, u32[]{:S(2)}) collective-permute-start(s32[2]{0:T(128)S(1)} %get-tuple-element.24), channel_id=1, source_target_pairs={{0,3},{1,0},{2,1},{3,2},{4,7},{5,4},{6,5},{7,6},{8,11},{9,8},{10,9... | collective-permute-start | bytes 32 | tf_op jit(solution)/shard_map/ppermute | solution.py:141
  37.6 5.7 %collective-permute-start.1 = (s32[2]{0:T(128)S(1)}, s32[2]{0:T(128)S(1)}, u32[]{:S(2)}, u32[]{:S(2)}) collective-permute-start(s32[2]{0:T(128)S(1)} %get-tuple-element.24), channel_id=1, source_target_pairs={{0,2},{1,3},{2,0},{3,1},{4,6},{5,7},{6,4},{7,5},{8,10},{9,11},{10,... | collective-permute-start | bytes 32 | tf_op jit(solution)/shard_map/ppermute | solution.py:141
  40.0 3.5 collective-permute-start.2
  72.0 15.3 %collective-permute-start.3 = (bf16[2,8,8,1152]{3,2,1,0:T(8,128)(2,1)}, bf16[2,8,8,1152]{3,2,1,0:T(8,128)(2,1)S(1)}, u32[]{:S(2)}, u32[]{:S(2)}) collective-permute-start(bf16[2,8,8,1152]{3,2,1,0:T(8,128)(2,1)} %get-tuple-element.43), channel_id=1, source_target_pairs={{0,3},{1,0},{2,1},{3,2},{4,7},{5,4},{6,5},{7,6},{8,11},{9,8},{10,9... | collective-permute-start | bytes 884744 | tf_op jit(solution)/shard_map/ppermute | solution.py:154
  78.3 54.4 %all-to-all-start.2 = ((bf16[8,8,16,2048]{3,2,1,0:T(8,128)(2,1)}), bf16[8,8,16,2048]{3,2,1,0:T(8,128)(2,1)}, u32[]{:S(2)}, u32[]{:S(2)}) async-start(bf16[8,8,16,2048]{3,2,1,0:T(8,128)(2,1)} %bitcast.154), calls=%async_computation.2 | async-start | bytes 8388608 | tf_op jit(solution)/shard_map/all_to_all | solution.py:20
  83.0 85.5 %reduce-scatter.3.cloned.1.call-start = ((), (), s32[]{:S(2)}) async-start(), calls=%async_computation.10 | async-start | bytes 1327104 | tf_op jit(solution)/shard_map/reduce_scatter | solution.py:167
  83.1 11.0 %collective-permute-start.4 = (bf16[2,8,8,1152]{3,2,1,0:T(8,128)(2,1)}, bf16[2,8,8,1152]{3,2,1,0:T(8,128)(2,1)S(1)}, u32[]{:S(2)}, u32[]{:S(2)}) collective-permute-start(bf16[2,8,8,1152]{3,2,1,0:T(8,128)(2,1)} %get-tuple-element.44), channel_id=1, source_target_pairs={{0,2},{1,3},{2,0},{3,1},{4,6},{5,7},{6,4},{7,5},{8,10},{9,11},{10,... | collective-permute-start | bytes 884744 | tf_op jit(solution)/shard_map/ppermute | solution.py:154
  85.5 15.0 %collective-permute-start.5 = (bf16[2,8,8,1152]{3,2,1,0:T(8,128)(2,1)S(1)}, bf16[2,8,8,1152]{3,2,1,0:T(8,128)(2,1)S(1)}, u32[]{:S(2)}, u32[]{:S(2)}) collective-permute-start(bf16[2,8,8,1152]{3,2,1,0:T(8,128)(2,1)S(1)} %copy-done.15), channel_id=1, source_target_pairs={{0,1},{1,2},{2,3},{3,0},{4,5},{5,6},{6,7},{7,4},{8,9},{9,10},{10,1... | collective-permute-start | bytes 884744 | tf_op jit(solution)/shard_map/ppermute | solution.py:154
  138.5 62.2 %all-to-all-start.3 = ((bf16[8,8,16,2048]{3,2,1,0:T(8,128)(2,1)}), bf16[8,8,16,2048]{3,2,1,0:T(8,128)(2,1)}, u32[]{:S(2)}, u32[]{:S(2)}) async-start(bf16[8,8,16,2048]{3,2,1,0:T(8,128)(2,1)} %bitcast.153), calls=%async_computation.3 | async-start | bytes 8388608 | tf_op jit(solution)/shard_map/all_to_all | solution.py:20
  143.2 134.6 %all-gather.6.cloned.1.call-start = ((), (), s32[]{:S(2)}) async-start(), calls=%async_computation.11 | async-start | bytes 5308416 | tf_op jit(solution)/shard_map/all_gather | solution.py:179
  168.5 26.4 %collective-permute-start.6 = (bf16[2,32,1152]{2,1,0:T(8,128)(2,1)}, bf16[2,32,1152]{2,1,0:T(8,128)(2,1)S(1)}, u32[]{:S(2)}, u32[]{:S(2)}) collective-permute-start(bf16[2,32,1152]{2,1,0:T(8,128)(2,1)} %bitcast.166), channel_id=1, source_target_pairs={{0,24},{8,0},{16,8},{24,16},{1,25},{9,1},{17,9},{25,17},{2,26},{10... | collective-permute-start | bytes 442376 | tf_op jit(solution)/shard_map/ppermute | solution.py:41
  171.3 25.2 %collective-permute-start.7 = (bf16[2,32,1152]{2,1,0:T(8,128)(2,1)}, bf16[2,32,1152]{2,1,0:T(8,128)(2,1)S(1)}, u32[]{:S(2)}, u32[]{:S(2)}) collective-permute-start(bf16[2,32,1152]{2,1,0:T(8,128)(2,1)} %bitcast.167), channel_id=1, source_target_pairs={{0,16},{8,24},{16,0},{24,8},{1,17},{9,25},{17,1},{25,9},{2,18},{10... | collective-permute-start | bytes 442376 | tf_op jit(solution)/shard_map/ppermute | solution.py:41
  172.1 26.7 %collective-permute-start.8 = (bf16[2,32,1152]{2,1,0:T(8,128)(2,1)}, bf16[2,32,1152]{2,1,0:T(8,128)(2,1)S(1)}, u32[]{:S(2)}, u32[]{:S(2)}) collective-permute-start(bf16[2,32,1152]{2,1,0:T(8,128)(2,1)} %bitcast.168), channel_id=1, source_target_pairs={{0,8},{8,16},{16,24},{24,0},{1,9},{9,17},{17,25},{25,1},{2,10},{10... | collective-permute-start | bytes 442376 | tf_op jit(solution)/shard_map/ppermute | solution.py:41
  207.0 16.0 %all-to-all-start.4 = ((f32[64,1,128]{2,1,0:T(1,128)}), f32[64,1,128]{2,1,0:T(1,128)S(1)}, u32[]{:S(2)}, u32[]{:S(2)}) async-start(f32[64,1,128]{2,1,0:T(1,128)} %bitcast.43), calls=%async_computation.5 | async-start | bytes 65536 | tf_op jit(solution)/shard_map/all_to_all | solution.py:20
  213.2 150.8 %reduce-scatter.5.cloned.1.call-start = ((), (), s32[]{:S(2)}) async-start(), calls=%async_computation.12 | async-start | bytes 4718592 | tf_op jit(solution)/shard_map/reduce_scatter | solution.py:197
  277.8 12.4 %collective-permute-start.9 = (bf16[2,1024,1152]{2,1,0:T(8,128)(2,1)}, bf16[2,1024,1152]{2,1,0:T(8,128)(2,1)}, u32[]{:S(2)}, u32[]{:S(2)}) collective-permute-start(bf16[2,1024,1152]{2,1,0:T(8,128)(2,1)} %all-gather.6.cloned.1.call-done), channel_id=1, source_target_pairs={{0,4},{4,0},{1,5},{5,1},{2,6},{6,2},{3,7},{7,3},{8,12},{12,8},{9,1... | collective-permute-start | bytes 14155784 | tf_op jit(solution)/shard_map/ppermute | solution.py:182
  331.8 31.2 %all-to-all-start.7 = ((f32[256,4,128]{2,1,0:T(4,128)}), f32[256,4,128]{2,1,0:T(4,128)S(1)}, u32[]{:S(2)}, u32[]{:S(2)}) async-start(f32[256,4,128]{2,1,0:T(4,128)} %broadcast_in_dim.189), calls=%async_computation.9 | async-start | bytes 1048576 | tf_op jit(solution)/shard_map/all_to_all | solution.py:20
  344.8 20.6 %copy-start.13 = (bf16[2048,64]{0,1:T(8,128)(2,1)S(1)}, bf16[2048,64]{0,1:T(8,128)(2,1)}, u32[]{:S(2)}) copy-start(bf16[2048,64]{0,1:T(8,128)(2,1)} %param.10) | copy-start | bytes 786436
  344.8 21.7 %copy-start.1 = (bf16[1,2048,384]{2,1,0:T(8,128)(2,1)S(1)}, bf16[1,2048,384]{2,1,0:T(8,128)(2,1)}, u32[]{:S(2)}) copy-start(bf16[1,2048,384]{2,1,0:T(8,128)(2,1)} %param.11) | copy-start | bytes 4718596
  (14 other events, 40.9 us)
Sparse Core Ops, SparseCore 0:
  9.8 58.8 all-gather.7
  70.5 53.5 all-gather.9
  132.9 35.6 reduce-scatter.2
  200.9 57.4 all-gather.5
  283.9 74.6 reduce-scatter.4
